TPU v7x, 512 devices: a whole 4x4x16 slice. The times are simulated.
512 devices in a mesh: blk: 16 (over x, y_hi, core), dp: 32 (over z, y_lo).
Axes of the slice: x: 4, y: 4 (y_hi: 2, y_lo: 2; y = y_hi * 2 + y_lo), z: 16, core: 2. Of those that a mesh axis runs over, the one named last changes fastest.
Arguments:
- inputs: bfloat16 [32768, 2048], P('dp'), may hold values from -6 to 6
- inducing: bfloat16 [2048, 2048], P('blk'), may hold values from -6 to 6
Outputs:
- gram_slab: float32 [2048, 2048], P(('blk', 'dp'))
All inputs are finite; a program needn't handle non-finite values.
Results may differ from a plain program's by a relative error of at most 0.0003.
Values may be sent and summed in bfloat16 or wider, within the bound.
A program may use at most 64 MiB of HBM per device.

v0:
```python
import jax
import jax.numpy as jnp
from jax import lax
from jax.sharding import PartitionSpec as P


def shifted(value, axis, steps):
    count = lax.axis_size(axis)
    pairs = [(source, (source + steps) % count) for source in range(count)]
    return lax.ppermute(value, axis, pairs)


def local(inputs, inducing):
    row_count = inputs.shape[0]
    feature_count = inputs.shape[1]
    block_rows = inducing.shape[0]
    group_size = lax.axis_size("blk")
    position = lax.axis_index("blk")

    def deposit(assembled, kernel_piece, step_index):
        offset = (position - step_index) % group_size * block_rows
        return lax.dynamic_update_slice_in_dim(assembled, kernel_piece, offset, 1)

    products = lax.dot_general(
        inputs, inducing, (((1,), (1,)), ((), ())), preferred_element_type=jnp.float32
    )
    own_kernel = (products * products * (1.0 / feature_count)).astype(jnp.bfloat16)
    assembled = jnp.zeros((row_count, block_rows * group_size), jnp.bfloat16)
    assembled = deposit(assembled, own_kernel, 0)

    def advance_kernel(step_index, loop_state):
        moving, assembled = loop_state
        moving = shifted(moving, "blk", 1)
        return (moving, deposit(assembled, moving, step_index))

    moving, assembled = lax.fori_loop(1, group_size, advance_kernel, (own_kernel, assembled))
    summed = lax.psum_scatter(
        lax.dot_general(
            own_kernel, assembled, (((0,), (0,)), ((), ())), preferred_element_type=jnp.float32
        ),
        "dp",
        scatter_dimension=0,
        tiled=True,
    )
    return summed * (1.0 / (row_count * lax.axis_size("dp")))


def solution(mesh):
    placed = (P("dp", None), P("blk", None))
    return jax.shard_map(
        local, mesh=mesh, in_specs=placed, out_specs=P(("blk", "dp"), None), check_vma=False
    )
```

profile of v0, /device:TPU:6, one launch (start us, length us, event | category | flops | bytes accessed | tf_op | source)
XLA Modules:
  0.0 471.5 jit_solution(13464863686766839251)
XLA Ops:
  10.3 1.9 copy-done.1
  12.2 162.9 %while.17 = (s32[]{:T(128)}, bf16[1024,128]{1,0:T(8,128)(2,1)S(1)}, bf16[1024,2048]{1,0:T(8,128)(2,1)}, s32[]{:T(128)}, s32[]{:T(128)}, /*index=5*/s32[]{:T(128)}, s32[]{:T(128)}, s32[]{:T(128)}, s32[]{:T(128)}, s32[]{:T(128)}) while((s32[]{:T(128)}, bf16[1024,128]{1,0:T(8,128)(2,1)S(1)}, bf16[1024,2048]{1,0:T(8,128)(2,1)}, s32[]{:T(128)}, ...), condition=%wide.region_1.2_spmd, body=%wide.region_0.1_spmd.sunk | while | flops 18 | bytes 2097464 | solution.py:36
  14.2 8.1 %collective-permute-done = bf16[1024,128]{1,0:T(8,128)(2,1)S(1)} collective-permute-done((bf16[1024,128]{1,0:T(8,128)(2,1)S(1)}, bf16[1024,128]{1,0:T(8,128)(2,1)S(1)}, u32[]{:S(2)}, u32[]{:S(2)}) %collective-permute-start) | collective-permute-done | bytes 262176 | tf_op jit(solution)/shard_map/while/body/eval_jaxpr/ppermute | solution.py:10
  25.0 8.1 %collective-permute-done = bf16[1024,128]{1,0:T(8,128)(2,1)S(1)} collective-permute-done((bf16[1024,128]{1,0:T(8,128)(2,1)S(1)}, bf16[1024,128]{1,0:T(8,128)(2,1)S(1)}, u32[]{:S(2)}, u32[]{:S(2)}) %collective-permute-start) | collective-permute-done | bytes 262176 | tf_op jit(solution)/shard_map/while/body/eval_jaxpr/ppermute | solution.py:10
  35.9 8.1 %collective-permute-done = bf16[1024,128]{1,0:T(8,128)(2,1)S(1)} collective-permute-done((bf16[1024,128]{1,0:T(8,128)(2,1)S(1)}, bf16[1024,128]{1,0:T(8,128)(2,1)S(1)}, u32[]{:S(2)}, u32[]{:S(2)}) %collective-permute-start) | collective-permute-done | bytes 262176 | tf_op jit(solution)/shard_map/while/body/eval_jaxpr/ppermute | solution.py:10
  46.8 8.1 %collective-permute-done = bf16[1024,128]{1,0:T(8,128)(2,1)S(1)} collective-permute-done((bf16[1024,128]{1,0:T(8,128)(2,1)S(1)}, bf16[1024,128]{1,0:T(8,128)(2,1)S(1)}, u32[]{:S(2)}, u32[]{:S(2)}) %collective-permute-start) | collective-permute-done | bytes 262176 | tf_op jit(solution)/shard_map/while/body/eval_jaxpr/ppermute | solution.py:10
  57.6 8.1 %collective-permute-done = bf16[1024,128]{1,0:T(8,128)(2,1)S(1)} collective-permute-done((bf16[1024,128]{1,0:T(8,128)(2,1)S(1)}, bf16[1024,128]{1,0:T(8,128)(2,1)S(1)}, u32[]{:S(2)}, u32[]{:S(2)}) %collective-permute-start) | collective-permute-done | bytes 262176 | tf_op jit(solution)/shard_map/while/body/eval_jaxpr/ppermute | solution.py:10
  68.5 8.1 %collective-permute-done = bf16[1024,128]{1,0:T(8,128)(2,1)S(1)} collective-permute-done((bf16[1024,128]{1,0:T(8,128)(2,1)S(1)}, bf16[1024,128]{1,0:T(8,128)(2,1)S(1)}, u32[]{:S(2)}, u32[]{:S(2)}) %collective-permute-start) | collective-permute-done | bytes 262176 | tf_op jit(solution)/shard_map/while/body/eval_jaxpr/ppermute | solution.py:10
  79.3 8.1 %collective-permute-done = bf16[1024,128]{1,0:T(8,128)(2,1)S(1)} collective-permute-done((bf16[1024,128]{1,0:T(8,128)(2,1)S(1)}, bf16[1024,128]{1,0:T(8,128)(2,1)S(1)}, u32[]{:S(2)}, u32[]{:S(2)}) %collective-permute-start) | collective-permute-done | bytes 262176 | tf_op jit(solution)/shard_map/while/body/eval_jaxpr/ppermute | solution.py:10
  90.2 8.1 %collective-permute-done = bf16[1024,128]{1,0:T(8,128)(2,1)S(1)} collective-permute-done((bf16[1024,128]{1,0:T(8,128)(2,1)S(1)}, bf16[1024,128]{1,0:T(8,128)(2,1)S(1)}, u32[]{:S(2)}, u32[]{:S(2)}) %collective-permute-start) | collective-permute-done | bytes 262176 | tf_op jit(solution)/shard_map/while/body/eval_jaxpr/ppermute | solution.py:10
  101.1 8.1 %collective-permute-done = bf16[1024,128]{1,0:T(8,128)(2,1)S(1)} collective-permute-done((bf16[1024,128]{1,0:T(8,128)(2,1)S(1)}, bf16[1024,128]{1,0:T(8,128)(2,1)S(1)}, u32[]{:S(2)}, u32[]{:S(2)}) %collective-permute-start) | collective-permute-done | bytes 262176 | tf_op jit(solution)/shard_map/while/body/eval_jaxpr/ppermute | solution.py:10
  111.9 8.1 %collective-permute-done = bf16[1024,128]{1,0:T(8,128)(2,1)S(1)} collective-permute-done((bf16[1024,128]{1,0:T(8,128)(2,1)S(1)}, bf16[1024,128]{1,0:T(8,128)(2,1)S(1)}, u32[]{:S(2)}, u32[]{:S(2)}) %collective-permute-start) | collective-permute-done | bytes 262176 | tf_op jit(solution)/shard_map/while/body/eval_jaxpr/ppermute | solution.py:10
  120.8 2.6 collective-permute-start
  123.5 7.4 %collective-permute-done = bf16[1024,128]{1,0:T(8,128)(2,1)S(1)} collective-permute-done((bf16[1024,128]{1,0:T(8,128)(2,1)S(1)}, bf16[1024,128]{1,0:T(8,128)(2,1)S(1)}, u32[]{:S(2)}, u32[]{:S(2)}) %collective-permute-start) | collective-permute-done | bytes 262176 | tf_op jit(solution)/shard_map/while/body/eval_jaxpr/ppermute | solution.py:10
  131.7 3.9 collective-permute-start
  135.6 6.2 %collective-permute-done = bf16[1024,128]{1,0:T(8,128)(2,1)S(1)} collective-permute-done((bf16[1024,128]{1,0:T(8,128)(2,1)S(1)}, bf16[1024,128]{1,0:T(8,128)(2,1)S(1)}, u32[]{:S(2)}, u32[]{:S(2)}) %collective-permute-start) | collective-permute-done | bytes 262176 | tf_op jit(solution)/shard_map/while/body/eval_jaxpr/ppermute | solution.py:10
  142.6 5.1 %collective-permute-start = (bf16[1024,128]{1,0:T(8,128)(2,1)S(1)}, bf16[1024,128]{1,0:T(8,128)(2,1)S(1)}, u32[]{:S(2)}, u32[]{:S(2)}) collective-permute-start(bf16[1024,128]{1,0:T(8,128)(2,1)S(1)} %get-tuple-element.163), channel_id=1, source_target_pairs={{0,32},{32,64},{64,96},{96,128},{128,160},{160,192},{192,224},{224... | collective-permute-start | bytes 786440 | tf_op jit(solution)/shard_map/while/body/eval_jaxpr/ppermute | solution.py:10
  147.7 5.0 %collective-permute-done = bf16[1024,128]{1,0:T(8,128)(2,1)S(1)} collective-permute-done((bf16[1024,128]{1,0:T(8,128)(2,1)S(1)}, bf16[1024,128]{1,0:T(8,128)(2,1)S(1)}, u32[]{:S(2)}, u32[]{:S(2)}) %collective-permute-start) | collective-permute-done | bytes 262176 | tf_op jit(solution)/shard_map/while/body/eval_jaxpr/ppermute | solution.py:10
  153.4 6.3 %collective-permute-start = (bf16[1024,128]{1,0:T(8,128)(2,1)S(1)}, bf16[1024,128]{1,0:T(8,128)(2,1)S(1)}, u32[]{:S(2)}, u32[]{:S(2)}) collective-permute-start(bf16[1024,128]{1,0:T(8,128)(2,1)S(1)} %get-tuple-element.163), channel_id=1, source_target_pairs={{0,32},{32,64},{64,96},{96,128},{128,160},{160,192},{192,224},{224... | collective-permute-start | bytes 786440 | tf_op jit(solution)/shard_map/while/body/eval_jaxpr/ppermute | solution.py:10
  159.7 3.8 collective-permute-done
  164.3 7.5 %collective-permute-start = (bf16[1024,128]{1,0:T(8,128)(2,1)S(1)}, bf16[1024,128]{1,0:T(8,128)(2,1)S(1)}, u32[]{:S(2)}, u32[]{:S(2)}) collective-permute-start(bf16[1024,128]{1,0:T(8,128)(2,1)S(1)} %get-tuple-element.163), channel_id=1, source_target_pairs={{0,32},{32,64},{64,96},{96,128},{128,160},{160,192},{192,224},{224... | collective-permute-start | bytes 786440 | tf_op jit(solution)/shard_map/while/body/eval_jaxpr/ppermute | solution.py:10
  171.8 2.6 collective-permute-done
  175.2 3.9 fusion.2
  181.0 282.2 %all-reduce.3.cloned.1.call-done = f32[128,2048]{1,0:T(8,128)} async-done(((f32[128,2048]{1,0:T(8,128)}), f32[128,2048]{1,0:T(8,128)}) %all-reduce.3.cloned.1.call-update) | async-done | bytes 1048592
  (52 shorter events, 37.2 us)
Async XLA Ops:
  6.5 1.0 copy-start
  6.5 456.7 %all-reduce.3.cloned.1.call-start = ((), (), s32[]{:S(2)}) async-start(), calls=%async_computation | async-start | bytes 2097152
  6.5 2.4 copy-start.2
  10.3 1.9 copy-start.1
  12.2 10.1 %collective-permute-start = (bf16[1024,128]{1,0:T(8,128)(2,1)S(1)}, bf16[1024,128]{1,0:T(8,128)(2,1)S(1)}, u32[]{:S(2)}, u32[]{:S(2)}) collective-permute-start(bf16[1024,128]{1,0:T(8,128)(2,1)S(1)} %get-tuple-element.163), channel_id=1, source_target_pairs={{0,32},{32,64},{64,96},{96,128},{128,160},{160,192},{192,224},{224... | collective-permute-start | bytes 786440 | tf_op jit(solution)/shard_map/while/body/eval_jaxpr/ppermute | solution.py:10
  23.1 10.1 %collective-permute-start = (bf16[1024,128]{1,0:T(8,128)(2,1)S(1)}, bf16[1024,128]{1,0:T(8,128)(2,1)S(1)}, u32[]{:S(2)}, u32[]{:S(2)}) collective-permute-start(bf16[1024,128]{1,0:T(8,128)(2,1)S(1)} %get-tuple-element.163), channel_id=1, source_target_pairs={{0,32},{32,64},{64,96},{96,128},{128,160},{160,192},{192,224},{224... | collective-permute-start | bytes 786440 | tf_op jit(solution)/shard_map/while/body/eval_jaxpr/ppermute | solution.py:10
  34.0 10.1 %collective-permute-start = (bf16[1024,128]{1,0:T(8,128)(2,1)S(1)}, bf16[1024,128]{1,0:T(8,128)(2,1)S(1)}, u32[]{:S(2)}, u32[]{:S(2)}) collective-permute-start(bf16[1024,128]{1,0:T(8,128)(2,1)S(1)} %get-tuple-element.163), channel_id=1, source_target_pairs={{0,32},{32,64},{64,96},{96,128},{128,160},{160,192},{192,224},{224... | collective-permute-start | bytes 786440 | tf_op jit(solution)/shard_map/while/body/eval_jaxpr/ppermute | solution.py:10
  44.8 10.1 %collective-permute-start = (bf16[1024,128]{1,0:T(8,128)(2,1)S(1)}, bf16[1024,128]{1,0:T(8,128)(2,1)S(1)}, u32[]{:S(2)}, u32[]{:S(2)}) collective-permute-start(bf16[1024,128]{1,0:T(8,128)(2,1)S(1)} %get-tuple-element.163), channel_id=1, source_target_pairs={{0,32},{32,64},{64,96},{96,128},{128,160},{160,192},{192,224},{224... | collective-permute-start | bytes 786440 | tf_op jit(solution)/shard_map/while/body/eval_jaxpr/ppermute | solution.py:10
  55.7 10.1 %collective-permute-start = (bf16[1024,128]{1,0:T(8,128)(2,1)S(1)}, bf16[1024,128]{1,0:T(8,128)(2,1)S(1)}, u32[]{:S(2)}, u32[]{:S(2)}) collective-permute-start(bf16[1024,128]{1,0:T(8,128)(2,1)S(1)} %get-tuple-element.163), channel_id=1, source_target_pairs={{0,32},{32,64},{64,96},{96,128},{128,160},{160,192},{192,224},{224... | collective-permute-start | bytes 786440 | tf_op jit(solution)/shard_map/while/body/eval_jaxpr/ppermute | solution.py:10
  66.5 10.1 %collective-permute-start = (bf16[1024,128]{1,0:T(8,128)(2,1)S(1)}, bf16[1024,128]{1,0:T(8,128)(2,1)S(1)}, u32[]{:S(2)}, u32[]{:S(2)}) collective-permute-start(bf16[1024,128]{1,0:T(8,128)(2,1)S(1)} %get-tuple-element.163), channel_id=1, source_target_pairs={{0,32},{32,64},{64,96},{96,128},{128,160},{160,192},{192,224},{224... | collective-permute-start | bytes 786440 | tf_op jit(solution)/shard_map/while/body/eval_jaxpr/ppermute | solution.py:10
  77.4 10.1 %collective-permute-start = (bf16[1024,128]{1,0:T(8,128)(2,1)S(1)}, bf16[1024,128]{1,0:T(8,128)(2,1)S(1)}, u32[]{:S(2)}, u32[]{:S(2)}) collective-permute-start(bf16[1024,128]{1,0:T(8,128)(2,1)S(1)} %get-tuple-element.163), channel_id=1, source_target_pairs={{0,32},{32,64},{64,96},{96,128},{128,160},{160,192},{192,224},{224... | collective-permute-start | bytes 786440 | tf_op jit(solution)/shard_map/while/body/eval_jaxpr/ppermute | solution.py:10
  88.2 10.1 %collective-permute-start = (bf16[1024,128]{1,0:T(8,128)(2,1)S(1)}, bf16[1024,128]{1,0:T(8,128)(2,1)S(1)}, u32[]{:S(2)}, u32[]{:S(2)}) collective-permute-start(bf16[1024,128]{1,0:T(8,128)(2,1)S(1)} %get-tuple-element.163), channel_id=1, source_target_pairs={{0,32},{32,64},{64,96},{96,128},{128,160},{160,192},{192,224},{224... | collective-permute-start | bytes 786440 | tf_op jit(solution)/shard_map/while/body/eval_jaxpr/ppermute | solution.py:10
  99.1 10.1 %collective-permute-start = (bf16[1024,128]{1,0:T(8,128)(2,1)S(1)}, bf16[1024,128]{1,0:T(8,128)(2,1)S(1)}, u32[]{:S(2)}, u32[]{:S(2)}) collective-permute-start(bf16[1024,128]{1,0:T(8,128)(2,1)S(1)} %get-tuple-element.163), channel_id=1, source_target_pairs={{0,32},{32,64},{64,96},{96,128},{128,160},{160,192},{192,224},{224... | collective-permute-start | bytes 786440 | tf_op jit(solution)/shard_map/while/body/eval_jaxpr/ppermute | solution.py:10
  110.0 10.1 %collective-permute-start = (bf16[1024,128]{1,0:T(8,128)(2,1)S(1)}, bf16[1024,128]{1,0:T(8,128)(2,1)S(1)}, u32[]{:S(2)}, u32[]{:S(2)}) collective-permute-start(bf16[1024,128]{1,0:T(8,128)(2,1)S(1)} %get-tuple-element.163), channel_id=1, source_target_pairs={{0,32},{32,64},{64,96},{96,128},{128,160},{160,192},{192,224},{224... | collective-permute-start | bytes 786440 | tf_op jit(solution)/shard_map/while/body/eval_jaxpr/ppermute | solution.py:10
  120.8 10.1 %collective-permute-start = (bf16[1024,128]{1,0:T(8,128)(2,1)S(1)}, bf16[1024,128]{1,0:T(8,128)(2,1)S(1)}, u32[]{:S(2)}, u32[]{:S(2)}) collective-permute-start(bf16[1024,128]{1,0:T(8,128)(2,1)S(1)} %get-tuple-element.163), channel_id=1, source_target_pairs={{0,32},{32,64},{64,96},{96,128},{128,160},{160,192},{192,224},{224... | collective-permute-start | bytes 786440 | tf_op jit(solution)/shard_map/while/body/eval_jaxpr/ppermute | solution.py:10
  131.7 10.1 %collective-permute-start = (bf16[1024,128]{1,0:T(8,128)(2,1)S(1)}, bf16[1024,128]{1,0:T(8,128)(2,1)S(1)}, u32[]{:S(2)}, u32[]{:S(2)}) collective-permute-start(bf16[1024,128]{1,0:T(8,128)(2,1)S(1)} %get-tuple-element.163), channel_id=1, source_target_pairs={{0,32},{32,64},{64,96},{96,128},{128,160},{160,192},{192,224},{224... | collective-permute-start | bytes 786440 | tf_op jit(solution)/shard_map/while/body/eval_jaxpr/ppermute | solution.py:10
  142.6 10.1 %collective-permute-start = (bf16[1024,128]{1,0:T(8,128)(2,1)S(1)}, bf16[1024,128]{1,0:T(8,128)(2,1)S(1)}, u32[]{:S(2)}, u32[]{:S(2)}) collective-permute-start(bf16[1024,128]{1,0:T(8,128)(2,1)S(1)} %get-tuple-element.163), channel_id=1, source_target_pairs={{0,32},{32,64},{64,96},{96,128},{128,160},{160,192},{192,224},{224... | collective-permute-start | bytes 786440 | tf_op jit(solution)/shard_map/while/body/eval_jaxpr/ppermute | solution.py:10
  153.4 10.1 %collective-permute-start = (bf16[1024,128]{1,0:T(8,128)(2,1)S(1)}, bf16[1024,128]{1,0:T(8,128)(2,1)S(1)}, u32[]{:S(2)}, u32[]{:S(2)}) collective-permute-start(bf16[1024,128]{1,0:T(8,128)(2,1)S(1)} %get-tuple-element.163), channel_id=1, source_target_pairs={{0,32},{32,64},{64,96},{96,128},{128,160},{160,192},{192,224},{224... | collective-permute-start | bytes 786440 | tf_op jit(solution)/shard_map/while/body/eval_jaxpr/ppermute | solution.py:10
  164.3 10.1 %collective-permute-start = (bf16[1024,128]{1,0:T(8,128)(2,1)S(1)}, bf16[1024,128]{1,0:T(8,128)(2,1)S(1)}, u32[]{:S(2)}, u32[]{:S(2)}) collective-permute-start(bf16[1024,128]{1,0:T(8,128)(2,1)S(1)} %get-tuple-element.163), channel_id=1, source_target_pairs={{0,32},{32,64},{64,96},{96,128},{128,160},{160,192},{192,224},{224... | collective-permute-start | bytes 786440 | tf_op jit(solution)/shard_map/while/body/eval_jaxpr/ppermute | solution.py:10
Sparse Core Ops, SparseCore 0:
  179.2 283.9 all-reduce.2
where the time goes:
time: 472 us
  waiting for transfers between devices  389 us (82%)
  starting transfers between devices  44.4 us (9%)
  local copies, waits for them, and re-layouts  17.2 us (4%)
  between operations  14.1 us (3%)
  matrix products  5.28 us (1%)
    unnamed x2, waiting for transfers between devices  282 us
    ppermute x15, waiting for transfers between devices, shifted(): return lax.ppermute(value, axis, pairs)  106 us
    ppermute x15, starting transfers between devices, shifted(): return lax.ppermute(value, axis, pairs)  44.4 us
    dynamic_update_slice x15, local copies, waits for them, and re-layouts, deposit(): return lax.dynamic_update_slice_in_dim(assembled, kernel_piece, offset, 1)  11.4 us
  transfers between devices with their start and end apart: 16, of which 16 were waited for; matrix products, arithmetic and copies ran while one was open for 0% of the time, Pallas kernels for 0%

commit v1 on v0

v1 whole, which is shorter than its diff:
```python
import jax
import jax.numpy as jnp
from jax import lax
from jax.experimental import pallas as pl
from jax.experimental.pallas import tpu as pltpu
from jax.sharding import PartitionSpec as P

ROWS = 1024
FEAT = 2048
BLOCK = 128
CHUNKS = 4
CHUNK = ROWS // CHUNKS
TOTAL = 32768
OWN, EDGE, SIDE, FAR = 0, 2, 4, 5


def kernel(
    inputs, inducing, out, x_buf, i_buf, pieces, tiles, parts, strips, landed,
    in_sem, send_k, recv_k, recv_e, send_e, send_a, recv_a, send_b, recv_b,
    round_c, round_h, round_l, round_x, round_z, round_w,
):
    blk, dp = lax.axis_index("blk"), lax.axis_index("dp")
    x, yh, c = blk // 4, blk // 2 % 2, blk % 2
    z, yl = dp // 2, dp % 2

    def block_of(x_, yh_, c_):
        return (x_ + 8) % 4 * 4 + yh_ * 2 + c_

    def group_of(z_, yl_):
        return (z_ + 32) % 16 * 2 + yl_

    def remote(src, dst, send, recv, device):
        return pltpu.make_async_remote_copy(
            src_ref=src, dst_ref=dst, send_sem=send, recv_sem=recv,
            device_id=device, device_id_type=pl.DeviceIdType.MESH,
        )

    def signal(sem, device):
        pl.semaphore_signal(sem, inc=1, device_id=device, device_id_type=pl.DeviceIdType.MESH)

    def wait_bytes(ref, sem):
        pltpu.make_async_copy(ref, ref, sem).wait()

    load_i = pltpu.make_async_copy(inducing, i_buf, in_sem.at[CHUNKS])
    load_i.start()
    loads = []
    for n in range(CHUNKS):
        rows = pl.ds(n * CHUNK, CHUNK)
        load = pltpu.make_async_copy(inputs.at[rows], x_buf.at[rows], in_sem.at[n])
        load.start()
        loads.append(load)

    partner = (block_of(x, yh, 1 - c), dp)
    edge = (block_of(x, 1 - yh, c), dp)
    beside = (blk, group_of(z, 1 - yl))
    line = [(block_of(x + s, yh, c), dp) for s in (1, 2, 3)]
    column = [(blk, group_of(z + s, l)) for s in (-2, -1, 1, 2) for l in (0, 1)]
    near = [partner, edge, beside] + line + column
    barrier = pltpu.get_barrier_semaphore()
    for device in near:
        signal(barrier, device)

    def make_chunk(n):
        rows = pl.ds(n * CHUNK, CHUNK)
        loads[n].wait()
        products = lax.dot_general(
            x_buf[rows, :], i_buf[...], (((1,), (1,)), ((), ())),
            preferred_element_type=jnp.float32,
        )
        pieces[OWN + c, rows, :] = (products * products * (1.0 / FEAT)).astype(jnp.bfloat16)

    def send_chunk(n):
        rows = pl.ds(n * CHUNK, CHUNK)
        own = pieces.at[OWN + c, rows]
        remote(own, pieces.at[OWN + c, rows], send_k, recv_k.at[0], partner).start()
        remote(own, pieces.at[EDGE + c, rows], send_k, recv_e.at[n], edge).start()
        remote(own, pieces.at[SIDE, rows], send_k, recv_k.at[1], line[2]).start()
        remote(own, pieces.at[FAR, rows], send_k, recv_k.at[2], line[1]).start()

    load_i.wait()
    make_chunk(0)
    pl.semaphore_wait(barrier, len(near))
    send_chunk(0)
    for n in range(1, CHUNKS):
        make_chunk(n)
        send_chunk(n)

    signal(round_c, partner)
    pl.semaphore_wait(round_c, 1)
    signal(round_h, edge)

    def gram(left, right):
        return lax.dot_general(
            pieces[left], pieces[right], (((0,), (0,)), ((), ())),
            preferred_element_type=jnp.float32,
        )

    def send_tile(k, place):
        reach = 1 + c
        step = (k % 4 - z + 16 + reach) % 4 - reach
        target = group_of(z + step, k // 4)
        slot = yl * 4 + step + reach
        src, dst = tiles.at[k if place == 0 else 8], parts.at[place, slot]

        @pl.when(target == dp)
        def _():
            pltpu.make_async_copy(src, dst, recv_a.at[place]).start()

        @pl.when(target != dp)
        def _():
            remote(src, dst, send_a.at[place], recv_a.at[place], (blk, target)).start()

    wait_bytes(pieces.at[0], recv_k.at[0])
    tiles[0] = gram(OWN + c, OWN)
    send_tile(0, 0)
    tiles[8] = gram(OWN + c, OWN + 1)
    send_tile(0, 1)

    pl.semaphore_wait(round_h, 1)
    signal(round_l, beside)

    for n in range(CHUNKS):
        rows = pl.ds(n * CHUNK, CHUNK)
        arrived = pieces.at[EDGE + c, rows]
        wait_bytes(arrived, recv_e.at[n])
        remote(arrived, arrived, send_e, recv_k.at[3], partner).start()
    tiles[5] = gram(EDGE + c, OWN + (c + yh) % 2)
    send_tile(5, 0)

    pl.semaphore_wait(round_l, 1)
    for device in line:
        signal(round_x, device)

    wait_bytes(pieces.at[0], recv_k.at[1])
    tiles[1] = gram(SIDE, OWN)
    send_tile(1, 0)
    tiles[2] = gram(SIDE, OWN + 1)
    send_tile(2, 0)

    pl.semaphore_wait(round_x, 3)
    for s in (-2, 2):
        signal(round_z, (blk, group_of(z + s, yl)))

    wait_bytes(pieces.at[0], recv_k.at[3])
    tiles[3] = gram(SIDE, EDGE)
    send_tile(3, 0)
    tiles[4] = gram(SIDE, EDGE + 1)
    send_tile(4, 0)

    pl.semaphore_wait(round_z, 2)
    for s in (-4, 4):
        signal(round_w, (blk, group_of(z + s, yl)))

    wait_bytes(pieces.at[0], recv_k.at[2])
    half = (c + x // 2) % 2
    tiles[6] = gram(FAR, OWN + half)
    send_tile(6, 0)
    tiles[7] = gram(FAR, EDGE + half)
    send_tile(7, 0)

    pl.semaphore_wait(round_w, 2)

    mine = yl * 4 + z % 4
    first = mine == 0

    def one(k, value):
        return jnp.where(mine == k, value, 0)

    own_0, own_1 = block_of(x, yh, 0), block_of(x, yh, 1)
    edge_0, edge_1 = block_of(x, 1 - yh, 0), block_of(x, 1 - yh, 1)
    side, far = block_of(x + 1, yh, c), block_of(x + 2, yh, c)
    row = (
        one(0, blk) + one(1, side) + one(2, side) + one(3, side) + one(4, side)
        + one(5, block_of(x, 1 - yh, c)) + one(6, far) + one(7, far)
    )
    col = (
        one(0, own_0) + one(1, own_0) + one(2, own_1) + one(3, edge_0) + one(4, edge_1)
        + one(5, block_of(x, yh, (c + yh) % 2)) + one(6, block_of(x, yh, half))
        + one(7, block_of(x, 1 - yh, half))
    )
    rows_of = (row, jnp.where(first, blk, col))
    cols_of = (col, jnp.where(first, own_1, row))

    def add_parts(place):
        total = parts[place, 0]
        for s in range(1, 8):
            total = total + parts[place, s]
        return total * (1.0 / TOTAL)

    def lay(place, value):
        for s in range(32):
            strips[place, s] = value[4 * s : 4 * s + 4]

    wait_bytes(parts.at[0], recv_a.at[0])
    tile = add_parts(0)
    lay(0, tile)

    @pl.when(first)
    def _():
        wait_bytes(parts.at[1], recv_a.at[1])
        lay(1, add_parts(1))

    @pl.when(jnp.logical_not(first))
    def _():
        lay(1, tile.T)

    def send_strips(n, carry):
        away = (8 - (n + 1) // 2) * (2 * (n % 2) - 1)
        w = (z + away + 32) % 16
        for l in (0, 1):
            for r in (0, 1):
                src = strips.at[r, w * 2 + l]
                dst = landed.at[z // 4 * 16 + cols_of[r]]
                target = w * 2 + l
                here = jnp.logical_and(target == dp, rows_of[r] == blk)

                @pl.when(here)
                def _():
                    pltpu.make_async_copy(src, dst, recv_b).start()

                @pl.when(jnp.logical_not(here))
                def _():
                    remote(src, dst, send_b.at[r], recv_b, (rows_of[r], target)).start()

        return carry

    lax.fori_loop(0, 16, send_strips, 0)

    wait_bytes(landed, recv_b)
    for g in range(16):
        out[:, g * BLOCK : (g + 1) * BLOCK] = (
            landed[g] + landed[16 + g] + landed[32 + g] + landed[48 + g]
        )

    wait_bytes(pieces.at[pl.ds(0, 4)], send_k)
    wait_bytes(pieces.at[0], send_e)
    wait_bytes(tiles.at[pl.ds(0, 7)], send_a.at[0])

    @pl.when(jnp.logical_not(first))
    def _():
        wait_bytes(tiles.at[0], send_a.at[1])

    for r in (0, 1):
        inside = rows_of[r] == blk

        @pl.when(inside)
        def _():
            wait_bytes(landed.at[pl.ds(0, 31)], send_b.at[r])

        @pl.when(jnp.logical_not(inside))
        def _():
            wait_bytes(landed.at[pl.ds(0, 32)], send_b.at[r])


def local(inputs, inducing):
    dma = pltpu.SemaphoreType.DMA
    regular = pltpu.SemaphoreType.REGULAR
    return pl.pallas_call(
        kernel,
        out_shape=jax.ShapeDtypeStruct((4, FEAT), jnp.float32),
        in_specs=[pl.BlockSpec(memory_space=pl.ANY)] * 2,
        out_specs=pl.BlockSpec(memory_space=pltpu.VMEM),
        scratch_shapes=[
            pltpu.VMEM((ROWS, FEAT), jnp.bfloat16),
            pltpu.VMEM((BLOCK, FEAT), jnp.bfloat16),
            pltpu.VMEM((6, ROWS, BLOCK), jnp.bfloat16),
            pltpu.VMEM((9, BLOCK, BLOCK), jnp.float32),
            pltpu.VMEM((2, 8, BLOCK, BLOCK), jnp.float32),
            pltpu.VMEM((2, 32, 4, BLOCK), jnp.float32),
            pltpu.VMEM((64, 4, BLOCK), jnp.float32),
            dma((CHUNKS + 1,)),
            dma,
            dma((4,)),
            dma((CHUNKS,)),
            dma,
            dma((2,)),
            dma((2,)),
            dma((2,)),
            dma,
            regular,
            regular,
            regular,
            regular,
            regular,
            regular,
        ],
        compiler_params=pltpu.CompilerParams(
            collective_id=0, has_side_effects=True, vmem_limit_bytes=48 * 1024 * 1024
        ),
    )(inputs, inducing)


def solution(mesh):
    placed = (P("dp", None), P("blk", None))
    return jax.shard_map(
        local, mesh=mesh, in_specs=placed, out_specs=P(("blk", "dp"), None), check_vma=False
    )
```

time: 472 us -> 53.5 us (0.11)
  the two profiles are of different devices: /device:TPU:6 before, /device:TPU:1 now
where the time goes in v1:
time: 53.5 us; the launch traced here: 53.3 us
  Pallas kernels  49.5 us (93%)
  local copies, waits for them, and re-layouts  3.85 us (7%)
    pallas_call x1, Pallas kernels, local(): pl.pallas_call(kernel, out_shape=jax.ShapeDtypeStruct((4, FEAT), jnp.floa...  49.5 us
    unnamed x5, local copies, waits for them, and re-layouts  3.85 us

profile of v1, /device:TPU:1, one launch (start us, length us, event | category | flops | bytes accessed | tf_op | source)
XLA Modules:
  0.0 53.3 jit_solution(12906876137577248084)
XLA Ops:
  0.0 0.0 copy-start
  0.0 2.2 %copy-done = bf16[1024,2048]{1,0:T(8,128)(2,1)S(1)} copy-done((bf16[1024,2048]{1,0:T(8,128)(2,1)S(1)}, bf16[1024,2048]{1,0:T(8,128)(2,1)}, u32[]{:S(2)}) %copy-start) | copy-done | bytes 4194328
  2.2 0.0 copy-start.1
  2.2 1.0 %copy-done.1 = bf16[128,2048]{1,0:T(8,128)(2,1)S(1)} copy-done((bf16[128,2048]{1,0:T(8,128)(2,1)S(1)}, bf16[128,2048]{1,0:T(8,128)(2,1)}, u32[]{:S(2)}) %copy-start.1) | copy-done | bytes 524312
  3.2 49.5 %shard_map.28 = f32[4,2048]{1,0:T(4,128)S(1)} custom-call(bf16[1024,2048]{1,0:T(8,128)(2,1)S(1)} %copy-done, bf16[128,2048]{1,0:T(8,128)(2,1)S(1)} %copy-done.1), custom_call_target="tpu_custom_call" | custom-call | tf_op jit(solution)/shard_map/pallas_call | solution.py:258
  52.7 0.6 %copy.4 = f32[4,2048]{1,0:T(4,128)} copy(f32[4,2048]{1,0:T(4,128)S(1)} %shard_map.28) | data formatting | bytes 65536
Async XLA Ops:
  0.0 2.2 %copy-start = (bf16[1024,2048]{1,0:T(8,128)(2,1)S(1)}, bf16[1024,2048]{1,0:T(8,128)(2,1)}, u32[]{:S(2)}) copy-start(bf16[1024,2048]{1,0:T(8,128)(2,1)} %inputs.1) | copy-start | bytes 12582916
  2.2 1.0 %copy-start.1 = (bf16[128,2048]{1,0:T(8,128)(2,1)S(1)}, bf16[128,2048]{1,0:T(8,128)(2,1)}, u32[]{:S(2)}) copy-start(bf16[128,2048]{1,0:T(8,128)(2,1)} %inducing.1) | copy-start | bytes 1572868

commit v2 on v1

--- a/solution.py
+++ b/solution.py
@@ -8,8 +8,8 @@
 ROWS = 1024
 FEAT = 2048
 BLOCK = 128
-CHUNKS = 4
-CHUNK = ROWS // CHUNKS
+CUTS = (0, 128, 384, 704, 1024)
+CHUNKS = len(CUTS) - 1
 TOTAL = 32768
 OWN, EDGE, SIDE, FAR = 0, 2, 4, 5
 
@@ -17,7 +17,7 @@
 def kernel(
     inputs, inducing, out, x_buf, i_buf, pieces, tiles, parts, strips, landed,
     in_sem, send_k, recv_k, recv_e, send_e, send_a, recv_a, send_b, recv_b,
-    round_c, round_h, round_l, round_x, round_z, round_w,
+    round_p, round_z, round_w,
 ):
     blk, dp = lax.axis_index("blk"), lax.axis_index("dp")
     x, yh, c = blk // 4, blk // 2 % 2, blk % 2
@@ -45,23 +45,25 @@
     load_i.start()
     loads = []
     for n in range(CHUNKS):
-        rows = pl.ds(n * CHUNK, CHUNK)
+        rows = pl.ds(CUTS[n], CUTS[n + 1] - CUTS[n])
         load = pltpu.make_async_copy(inputs.at[rows], x_buf.at[rows], in_sem.at[n])
         load.start()
         loads.append(load)
 
     partner = (block_of(x, yh, 1 - c), dp)
     edge = (block_of(x, 1 - yh, c), dp)
+    across = (block_of(x, 1 - yh, 1 - c), dp)
     beside = (blk, group_of(z, 1 - yl))
     line = [(block_of(x + s, yh, c), dp) for s in (1, 2, 3)]
     column = [(blk, group_of(z + s, l)) for s in (-2, -1, 1, 2) for l in (0, 1)]
-    near = [partner, edge, beside] + line + column
+    plane = [partner, edge, across] + line
+    near = plane + [beside] + column
     barrier = pltpu.get_barrier_semaphore()
     for device in near:
         signal(barrier, device)
 
     def make_chunk(n):
-        rows = pl.ds(n * CHUNK, CHUNK)
+        rows = pl.ds(CUTS[n], CUTS[n + 1] - CUTS[n])
         loads[n].wait()
         products = lax.dot_general(
             x_buf[rows, :], i_buf[...], (((1,), (1,)), ((), ())),
@@ -70,35 +72,48 @@
         pieces[OWN + c, rows, :] = (products * products * (1.0 / FEAT)).astype(jnp.bfloat16)
 
     def send_chunk(n):
-        rows = pl.ds(n * CHUNK, CHUNK)
+        rows = pl.ds(CUTS[n], CUTS[n + 1] - CUTS[n])
         own = pieces.at[OWN + c, rows]
-        remote(own, pieces.at[OWN + c, rows], send_k, recv_k.at[0], partner).start()
-        remote(own, pieces.at[EDGE + c, rows], send_k, recv_e.at[n], edge).start()
-        remote(own, pieces.at[SIDE, rows], send_k, recv_k.at[1], line[2]).start()
-        remote(own, pieces.at[FAR, rows], send_k, recv_k.at[2], line[1]).start()
+        remote(own, pieces.at[OWN + c, rows], send_k.at[0], recv_k.at[0], partner).start()
+        remote(own, pieces.at[SIDE, rows], send_k.at[1], recv_k.at[1], line[2]).start()
+        remote(own, pieces.at[EDGE + c, rows], send_k.at[2], recv_e.at[n], edge).start()
+
+        @pl.when(x % 2 == 0)
+        def _():
+            remote(own, pieces.at[FAR, rows], send_k.at[3], recv_k.at[2], line[1]).start()
+
+    def send_far():
+        wait_bytes(pieces.at[0], send_k.at[1])
+        remote(pieces.at[OWN + c], pieces.at[FAR], send_k.at[3], recv_k.at[2], line[1]).start()
 
     load_i.wait()
     make_chunk(0)
     pl.semaphore_wait(barrier, len(near))
     send_chunk(0)
+    for device in plane:
+        signal(round_p, device)
     for n in range(1, CHUNKS):
         make_chunk(n)
         send_chunk(n)
 
-    signal(round_c, partner)
-    pl.semaphore_wait(round_c, 1)
-    signal(round_h, edge)
-
-    def gram(left, right):
-        return lax.dot_general(
-            pieces[left], pieces[right], (((0,), (0,)), ((), ())),
-            preferred_element_type=jnp.float32,
-        )
+    pl.semaphore_wait(round_p, len(plane))
+    for s in (-2, 2):
+        signal(round_z, (blk, group_of(z + s, yl)))
+
+    def gram(left, *rights):
+        turned = pieces[left].T
+        return [
+            lax.dot_general(
+                turned, pieces[right], (((1,), (0,)), ((), ())),
+                preferred_element_type=jnp.float32,
+            )
+            for right in rights
+        ]
 
     def send_tile(k, place):
         reach = 1 + c
-        step = (k % 4 - z + 16 + reach) % 4 - reach
-        target = group_of(z + step, k // 4)
+        step = (k + 2 * c - z + 16 + reach) % 4 - reach
+        target = group_of(z + step, (k // 4 + c) % 2)
         slot = yl * 4 + step + reach
         src, dst = tiles.at[k if place == 0 else 8], parts.at[place, slot]
 
@@ -111,56 +126,45 @@
             remote(src, dst, send_a.at[place], recv_a.at[place], (blk, target)).start()
 
     wait_bytes(pieces.at[0], recv_k.at[0])
-    tiles[0] = gram(OWN + c, OWN)
+    tiles[0], tiles[8] = gram(OWN + c, OWN, OWN + 1)
     send_tile(0, 0)
-    tiles[8] = gram(OWN + c, OWN + 1)
     send_tile(0, 1)
 
-    pl.semaphore_wait(round_h, 1)
-    signal(round_l, beside)
+    @pl.when(x % 2 == 1)
+    def _():
+        send_far()
 
     for n in range(CHUNKS):
-        rows = pl.ds(n * CHUNK, CHUNK)
+        rows = pl.ds(CUTS[n], CUTS[n + 1] - CUTS[n])
         arrived = pieces.at[EDGE + c, rows]
         wait_bytes(arrived, recv_e.at[n])
         remote(arrived, arrived, send_e, recv_k.at[3], partner).start()
-    tiles[5] = gram(EDGE + c, OWN + (c + yh) % 2)
-    send_tile(5, 0)
-
-    pl.semaphore_wait(round_l, 1)
-    for device in line:
-        signal(round_x, device)
-
-    wait_bytes(pieces.at[0], recv_k.at[1])
-    tiles[1] = gram(SIDE, OWN)
-    send_tile(1, 0)
-    tiles[2] = gram(SIDE, OWN + 1)
-    send_tile(2, 0)
-
-    pl.semaphore_wait(round_x, 3)
-    for s in (-2, 2):
-        signal(round_z, (blk, group_of(z + s, yl)))
-
-    wait_bytes(pieces.at[0], recv_k.at[3])
-    tiles[3] = gram(SIDE, EDGE)
-    send_tile(3, 0)
-    tiles[4] = gram(SIDE, EDGE + 1)
-    send_tile(4, 0)
 
     pl.semaphore_wait(round_z, 2)
     for s in (-4, 4):
         signal(round_w, (blk, group_of(z + s, yl)))
 
+    wait_bytes(pieces.at[0], recv_k.at[1])
+    tiles[2], tiles[7] = gram(SIDE, OWN, OWN + 1)
+    send_tile(2, 0)
+    send_tile(7, 0)
+    (tiles[5],) = gram(EDGE + c, OWN + (c + yh) % 2)
+    send_tile(5, 0)
+
+    wait_bytes(pieces.at[0], recv_k.at[3])
+    tiles[4], tiles[1] = gram(SIDE, EDGE, EDGE + 1)
+    send_tile(4, 0)
+    send_tile(1, 0)
+
     wait_bytes(pieces.at[0], recv_k.at[2])
     half = (c + x // 2) % 2
-    tiles[6] = gram(FAR, OWN + half)
+    tiles[6], tiles[3] = gram(FAR, OWN + half, EDGE + half)
     send_tile(6, 0)
-    tiles[7] = gram(FAR, EDGE + half)
-    send_tile(7, 0)
+    send_tile(3, 0)
 
     pl.semaphore_wait(round_w, 2)
 
-    mine = yl * 4 + z % 4
+    mine = (yl + c) % 2 * 4 + (z + 2 * c) % 4
     first = mine == 0
 
     def one(k, value):
@@ -170,13 +174,13 @@
     edge_0, edge_1 = block_of(x, 1 - yh, 0), block_of(x, 1 - yh, 1)
     side, far = block_of(x + 1, yh, c), block_of(x + 2, yh, c)
     row = (
-        one(0, blk) + one(1, side) + one(2, side) + one(3, side) + one(4, side)
-        + one(5, block_of(x, 1 - yh, c)) + one(6, far) + one(7, far)
+        one(0, blk) + one(2, side) + one(7, side) + one(4, side) + one(1, side)
+        + one(5, block_of(x, 1 - yh, c)) + one(6, far) + one(3, far)
     )
     col = (
-        one(0, own_0) + one(1, own_0) + one(2, own_1) + one(3, edge_0) + one(4, edge_1)
+        one(0, own_0) + one(2, own_0) + one(7, own_1) + one(4, edge_0) + one(1, edge_1)
         + one(5, block_of(x, yh, (c + yh) % 2)) + one(6, block_of(x, yh, half))
-        + one(7, block_of(x, 1 - yh, half))
+        + one(3, block_of(x, 1 - yh, half))
     )
     rows_of = (row, jnp.where(first, blk, col))
     cols_of = (col, jnp.where(first, own_1, row))
@@ -205,8 +209,7 @@
         lay(1, tile.T)
 
     def send_strips(n, carry):
-        away = (8 - (n + 1) // 2) * (2 * (n % 2) - 1)
-        w = (z + away + 32) % 16
+        w = n + n // 8 * (23 - 2 * n)
         for l in (0, 1):
             for r in (0, 1):
                 src = strips.at[r, w * 2 + l]
@@ -232,7 +235,13 @@
             landed[g] + landed[16 + g] + landed[32 + g] + landed[48 + g]
         )
 
-    wait_bytes(pieces.at[pl.ds(0, 4)], send_k)
+    for n in (0, 2, 3):
+        wait_bytes(pieces.at[0], send_k.at[n])
+
+    @pl.when(x % 2 == 0)
+    def _():
+        wait_bytes(pieces.at[0], send_k.at[1])
+
     wait_bytes(pieces.at[0], send_e)
     wait_bytes(tiles.at[pl.ds(0, 7)], send_a.at[0])
 
@@ -269,7 +278,7 @@
             pltpu.VMEM((2, 32, 4, BLOCK), jnp.float32),
             pltpu.VMEM((64, 4, BLOCK), jnp.float32),
             dma((CHUNKS + 1,)),
-            dma,
+            dma((4,)),
             dma((4,)),
             dma((CHUNKS,)),
             dma,
@@ -280,12 +289,9 @@
             regular,
             regular,
             regular,
-            regular,
-            regular,
-            regular,
         ],
         compiler_params=pltpu.CompilerParams(
-            collective_id=0, has_side_effects=True, vmem_limit_bytes=48 * 1024 * 1024
+            collective_id=0, has_side_effects=True, vmem_limit_bytes=215 * 256 * 1024
         ),
     )(inputs, inducing)
 

time: 53.5 us -> 46.6 us (0.87); the launches traced: 53.3 us -> 45.9 us
  Pallas kernels: 49.5 us -> 45.2 us
  local copies, waits for them, and re-layouts: 3.85 us -> 0.62 us
    pallas_call x1, Pallas kernels: 49.5 us -> 45.2 us  [local(): pl.pallas_call(kernel, out_shape=jax.ShapeDtypeStruct((4, FEAT), jnp.floa...]
    unnamed x5 -> x1, local copies, waits for them, and re-layouts: 3.85 us -> 0.62 us
where the time goes in v2:
time: 46.6 us; the launch traced here: 45.9 us
  Pallas kernels  45.2 us (97%)
  local copies, waits for them, and re-layouts  0.62 us (1%)
    pallas_call x1, Pallas kernels, local(): pl.pallas_call(kernel, out_shape=jax.ShapeDtypeStruct((4, FEAT), jnp.floa...  45.2 us

profile of v2, /device:TPU:1, one launch (start us, length us, event | category | flops | bytes accessed | tf_op | source)
XLA Modules:
  0.0 45.9 jit_solution(1551659772494881856)
XLA Ops:
  0.0 45.2 %shard_map.28 = f32[4,2048]{1,0:T(4,128)S(1)} custom-call(bf16[1024,2048]{1,0:T(8,128)(2,1)} %inputs.1, bf16[128,2048]{1,0:T(8,128)(2,1)} %inducing.1), custom_call_target="tpu_custom_call" | custom-call | tf_op jit(solution)/shard_map/pallas_call | solution.py:267
  45.3 0.6 %copy.4 = f32[4,2048]{1,0:T(4,128)} copy(f32[4,2048]{1,0:T(4,128)S(1)} %shard_map.28) | data formatting | bytes 65536

commit v3 on v2

--- a/solution.py
+++ b/solution.py
@@ -15,8 +15,8 @@
 
 
 def kernel(
-    inputs, inducing, out, x_buf, i_buf, pieces, tiles, parts, strips, landed,
-    in_sem, send_k, recv_k, recv_e, send_e, send_a, recv_a, send_b, recv_b,
+    inputs, inducing, out, x_buf, i_buf, pieces, tiles, parts, sums, strips, landed,
+    in_sem, send_k, recv_k, recv_e, send_e, send_a, recv_a, send_u, send_b, recv_b,
     round_p, round_z, round_w,
 ):
     blk, dp = lax.axis_index("blk"), lax.axis_index("dp")
@@ -110,20 +110,28 @@
             for right in rights
         ]
 
+    reach = 1 + c
+    meets = (yl + c + 1) % 2
+    middle = z % 4 == 2 * c
+
     def send_tile(k, place):
-        reach = 1 + c
         step = (k + 2 * c - z + 16 + reach) % 4 - reach
-        target = group_of(z + step, (k // 4 + c) % 2)
-        slot = yl * 4 + step + reach
-        src, dst = tiles.at[k if place == 0 else 8], parts.at[place, slot]
+        if k == 0:
+            target = group_of(z + step, yl)
+            dst = parts.at[meets * place + 1 - meets, (meets * yl + (1 - meets) * place) * 4 + step + reach]
+            recv = recv_a.at[meets * place + (1 - meets) * 2]
+        else:
+            target = group_of(z + step, (k // 4 + c) % 2)
+            dst, recv = parts.at[0, yl * 4 + step + reach], recv_a.at[0]
+        src = tiles.at[8 if place else k]
 
         @pl.when(target == dp)
         def _():
-            pltpu.make_async_copy(src, dst, recv_a.at[place]).start()
+            pltpu.make_async_copy(src, dst, recv).start()
 
         @pl.when(target != dp)
         def _():
-            remote(src, dst, send_a.at[place], recv_a.at[place], (blk, target)).start()
+            remote(src, dst, send_a.at[place], recv, (blk, target)).start()
 
     wait_bytes(pieces.at[0], recv_k.at[0])
     tiles[0], tiles[8] = gram(OWN + c, OWN, OWN + 1)
@@ -155,6 +163,20 @@
     tiles[4], tiles[1] = gram(SIDE, EDGE, EDGE + 1)
     send_tile(4, 0)
     send_tile(1, 0)
+
+    between = jnp.logical_and(middle, meets == 0)
+
+    @pl.when(between)
+    def _():
+        wait_bytes(parts.at[1], recv_a.at[2])
+        for place in (0, 1):
+            sums[place] = (
+                parts[1, place * 4] + parts[1, place * 4 + 1]
+                + parts[1, place * 4 + 2] + parts[1, place * 4 + 3]
+            )
+            remote(
+                sums.at[place], parts.at[place, (1 - c) * 4], send_u, recv_a.at[place], beside
+            ).start()
 
     wait_bytes(pieces.at[0], recv_k.at[2])
     half = (c + x // 2) % 2
@@ -185,9 +207,9 @@
     rows_of = (row, jnp.where(first, blk, col))
     cols_of = (col, jnp.where(first, own_1, row))
 
-    def add_parts(place):
-        total = parts[place, 0]
-        for s in range(1, 8):
+    def add_parts(place, slots):
+        total = parts[place, slots[0]]
+        for s in slots[1:]:
             total = total + parts[place, s]
         return total * (1.0 / TOTAL)
 
@@ -195,17 +217,17 @@
         for s in range(32):
             strips[place, s] = value[4 * s : 4 * s + 4]
 
-    wait_bytes(parts.at[0], recv_a.at[0])
-    tile = add_parts(0)
-    lay(0, tile)
-
     @pl.when(first)
     def _():
-        wait_bytes(parts.at[1], recv_a.at[1])
-        lay(1, add_parts(1))
+        for place in (0, 1):
+            wait_bytes(parts.at[place, pl.ds(0, 5)], recv_a.at[place])
+            lay(place, add_parts(place, [(1 - c) * 4] + [c * 4 + s for s in range(4)]))
 
     @pl.when(jnp.logical_not(first))
     def _():
+        wait_bytes(parts.at[0], recv_a.at[0])
+        tile = add_parts(0, range(8))
+        lay(0, tile)
         lay(1, tile.T)
 
     def send_strips(n, carry):
@@ -243,9 +265,16 @@
         wait_bytes(pieces.at[0], send_k.at[1])
 
     wait_bytes(pieces.at[0], send_e)
-    wait_bytes(tiles.at[pl.ds(0, 7)], send_a.at[0])
-
-    @pl.when(jnp.logical_not(first))
+    @pl.when(between)
+    def _():
+        wait_bytes(tiles.at[pl.ds(0, 6)], send_a.at[0])
+        wait_bytes(sums, send_u)
+
+    @pl.when(jnp.logical_not(between))
+    def _():
+        wait_bytes(tiles.at[pl.ds(0, 7)], send_a.at[0])
+
+    @pl.when(jnp.logical_not(middle))
     def _():
         wait_bytes(tiles.at[0], send_a.at[1])
 
@@ -275,6 +304,7 @@
             pltpu.VMEM((6, ROWS, BLOCK), jnp.bfloat16),
             pltpu.VMEM((9, BLOCK, BLOCK), jnp.float32),
             pltpu.VMEM((2, 8, BLOCK, BLOCK), jnp.float32),
+            pltpu.VMEM((2, BLOCK, BLOCK), jnp.float32),
             pltpu.VMEM((2, 32, 4, BLOCK), jnp.float32),
             pltpu.VMEM((64, 4, BLOCK), jnp.float32),
             dma((CHUNKS + 1,)),
@@ -283,7 +313,8 @@
             dma((CHUNKS,)),
             dma,
             dma((2,)),
-            dma((2,)),
+            dma((3,)),
+            dma,
             dma((2,)),
             dma,
             regular,

time: 46.6 us -> 44.8 us (0.961)
  the two profiles are of different devices: /device:TPU:1 before, /device:TPU:2 now
where the time goes in v3:
time: 44.8 us; the launch traced here: 44.7 us
  Pallas kernels  44.1 us (98%)
  local copies, waits for them, and re-layouts  0.62 us (1%)
    pallas_call x1, Pallas kernels, local(): pl.pallas_call(kernel, out_shape=jax.ShapeDtypeStruct((4, FEAT), jnp.floa...  44.1 us

profile of v3, /device:TPU:2, one launch (start us, length us, event | category | flops | bytes accessed | tf_op | source)
XLA Modules:
  0.0 44.7 jit_solution(13333641964868881774)
XLA Ops:
  0.0 44.1 %shard_map.28 = f32[4,2048]{1,0:T(4,128)S(1)} custom-call(bf16[1024,2048]{1,0:T(8,128)(2,1)} %inputs.1, bf16[128,2048]{1,0:T(8,128)(2,1)} %inducing.1), custom_call_target="tpu_custom_call" | custom-call | tf_op jit(solution)/shard_map/pallas_call | solution.py:296
  44.1 0.6 %copy.4 = f32[4,2048]{1,0:T(4,128)} copy(f32[4,2048]{1,0:T(4,128)S(1)} %shard_map.28) | data formatting | bytes 65536

commit v4 on v3

--- a/solution.py
+++ b/solution.py
@@ -8,15 +8,17 @@
 ROWS = 1024
 FEAT = 2048
 BLOCK = 128
-CUTS = (0, 128, 384, 704, 1024)
+CUTS = (0, 128, 256, 640, 1024)
 CHUNKS = len(CUTS) - 1
+PASSED = 2
+HALF = CUTS[PASSED]
 TOTAL = 32768
 OWN, EDGE, SIDE, FAR = 0, 2, 4, 5
 
 
 def kernel(
-    inputs, inducing, out, x_buf, i_buf, pieces, tiles, parts, sums, strips, landed,
-    in_sem, send_k, recv_k, recv_e, send_e, send_a, recv_a, send_u, send_b, recv_b,
+    inputs, inducing, out, x_buf, i_buf, pieces, passing, tiles, parts, sums, strips, landed,
+    in_sem, send_k, recv_k, send_p, recv_p, recv_e, send_e, send_a, recv_a, send_u, send_b, recv_b,
     round_p, round_z, round_w,
 ):
     blk, dp = lax.axis_index("blk"), lax.axis_index("dp")
@@ -78,13 +80,28 @@
         remote(own, pieces.at[SIDE, rows], send_k.at[1], recv_k.at[1], line[2]).start()
         remote(own, pieces.at[EDGE + c, rows], send_k.at[2], recv_e.at[n], edge).start()
 
+        if n < PASSED:
+
+            @pl.when(x % 2 == 1)
+            def _():
+                remote(own, passing.at[rows], send_p, recv_p.at[n], line[0]).start()
+
+    def send_far():
         @pl.when(x % 2 == 0)
         def _():
-            remote(own, pieces.at[FAR, rows], send_k.at[3], recv_k.at[2], line[1]).start()
-
-    def send_far():
-        wait_bytes(pieces.at[0], send_k.at[1])
-        remote(pieces.at[OWN + c], pieces.at[FAR], send_k.at[3], recv_k.at[2], line[1]).start()
+            remote(pieces.at[OWN + c], pieces.at[FAR], send_k.at[3], recv_k.at[2], line[1]).start()
+            for n in range(PASSED):
+                rows = pl.ds(CUTS[n], CUTS[n + 1] - CUTS[n])
+                wait_bytes(passing.at[rows], recv_p.at[n])
+                remote(passing.at[rows], pieces.at[FAR, rows], send_p, recv_k.at[2], line[0]).start()
+
+        @pl.when(x % 2 == 1)
+        def _():
+            wait_bytes(pieces.at[0], send_k.at[1])
+            rows = pl.ds(HALF, ROWS - HALF)
+            remote(
+                pieces.at[OWN + c, rows], pieces.at[FAR, rows], send_k.at[3], recv_k.at[2], line[1]
+            ).start()
 
     load_i.wait()
     make_chunk(0)
@@ -138,9 +155,7 @@
     send_tile(0, 0)
     send_tile(0, 1)
 
-    @pl.when(x % 2 == 1)
-    def _():
-        send_far()
+    send_far()
 
     for n in range(CHUNKS):
         rows = pl.ds(CUTS[n], CUTS[n + 1] - CUTS[n])
@@ -257,12 +272,18 @@
             landed[g] + landed[16 + g] + landed[32 + g] + landed[48 + g]
         )
 
-    for n in (0, 2, 3):
+    for n in (0, 2):
         wait_bytes(pieces.at[0], send_k.at[n])
+    wait_bytes(passing, send_p)
 
     @pl.when(x % 2 == 0)
     def _():
         wait_bytes(pieces.at[0], send_k.at[1])
+        wait_bytes(pieces.at[0], send_k.at[3])
+
+    @pl.when(x % 2 == 1)
+    def _():
+        wait_bytes(pieces.at[0, pl.ds(HALF, ROWS - HALF)], send_k.at[3])
 
     wait_bytes(pieces.at[0], send_e)
     @pl.when(between)
@@ -302,6 +323,7 @@
             pltpu.VMEM((ROWS, FEAT), jnp.bfloat16),
             pltpu.VMEM((BLOCK, FEAT), jnp.bfloat16),
             pltpu.VMEM((6, ROWS, BLOCK), jnp.bfloat16),
+            pltpu.VMEM((HALF, BLOCK), jnp.bfloat16),
             pltpu.VMEM((9, BLOCK, BLOCK), jnp.float32),
             pltpu.VMEM((2, 8, BLOCK, BLOCK), jnp.float32),
             pltpu.VMEM((2, BLOCK, BLOCK), jnp.float32),
@@ -310,6 +332,8 @@
             dma((CHUNKS + 1,)),
             dma((4,)),
             dma((4,)),
+            dma,
+            dma((PASSED,)),
             dma((CHUNKS,)),
             dma,
             dma((2,)),

time: 44.8 us -> 41.6 us (0.929)
  the two profiles are of different devices: /device:TPU:2 before, /device:TPU:1 now
where the time goes in v4:
time: 41.6 us; the launch traced here: 41.4 us
  Pallas kernels  40.8 us (98%)
  local copies, waits for them, and re-layouts  0.62 us (1%)
    pallas_call x1, Pallas kernels, local(): pl.pallas_call(kernel, out_shape=jax.ShapeDtypeStruct((4, FEAT), jnp.floa...  40.8 us

profile of v4, /device:TPU:1, one launch (start us, length us, event | category | flops | bytes accessed | tf_op | source)
XLA Modules:
  0.0 41.4 jit_solution(11368993338232158575)
XLA Ops:
  0.0 40.8 %shard_map.28 = f32[4,2048]{1,0:T(4,128)S(1)} custom-call(bf16[1024,2048]{1,0:T(8,128)(2,1)} %inputs.1, bf16[128,2048]{1,0:T(8,128)(2,1)} %inducing.1), custom_call_target="tpu_custom_call" | custom-call | tf_op jit(solution)/shard_map/pallas_call | solution.py:317
  40.8 0.6 %copy.4 = f32[4,2048]{1,0:T(4,128)} copy(f32[4,2048]{1,0:T(4,128)S(1)} %shard_map.28) | data formatting | bytes 65536

commit v5 on v4

--- a/solution.py
+++ b/solution.py
@@ -42,15 +42,6 @@
 
     def wait_bytes(ref, sem):
         pltpu.make_async_copy(ref, ref, sem).wait()
-
-    load_i = pltpu.make_async_copy(inducing, i_buf, in_sem.at[CHUNKS])
-    load_i.start()
-    loads = []
-    for n in range(CHUNKS):
-        rows = pl.ds(CUTS[n], CUTS[n + 1] - CUTS[n])
-        load = pltpu.make_async_copy(inputs.at[rows], x_buf.at[rows], in_sem.at[n])
-        load.start()
-        loads.append(load)
 
     partner = (block_of(x, yh, 1 - c), dp)
     edge = (block_of(x, 1 - yh, c), dp)
@@ -64,6 +55,15 @@
     for device in near:
         signal(barrier, device)
 
+    load_i = pltpu.make_async_copy(inducing, i_buf, in_sem.at[CHUNKS])
+    load_i.start()
+    loads = []
+    for n in range(CHUNKS):
+        rows = pl.ds(CUTS[n], CUTS[n + 1] - CUTS[n])
+        load = pltpu.make_async_copy(inputs.at[rows], x_buf.at[rows], in_sem.at[n])
+        load.start()
+        loads.append(load)
+
     def make_chunk(n):
         rows = pl.ds(CUTS[n], CUTS[n + 1] - CUTS[n])
         loads[n].wait()
@@ -104,18 +104,15 @@
             ).start()
 
     load_i.wait()
-    make_chunk(0)
+    for n in range(1):
+        make_chunk(n)
     pl.semaphore_wait(barrier, len(near))
-    send_chunk(0)
+    for n in range(CHUNKS):
+        if n >= 1:
+            make_chunk(n)
+        send_chunk(n)
     for device in plane:
         signal(round_p, device)
-    for n in range(1, CHUNKS):
-        make_chunk(n)
-        send_chunk(n)
-
-    pl.semaphore_wait(round_p, len(plane))
-    for s in (-2, 2):
-        signal(round_z, (blk, group_of(z + s, yl)))
 
     def gram(left, *rights):
         turned = pieces[left].T
@@ -156,6 +153,10 @@
     send_tile(0, 1)
 
     send_far()
+
+    pl.semaphore_wait(round_p, len(plane))
+    for s in (-2, 2):
+        signal(round_z, (blk, group_of(z + s, yl)))
 
     for n in range(CHUNKS):
         rows = pl.ds(CUTS[n], CUTS[n + 1] - CUTS[n])

time: 41.6 us -> 41.5 us (level)
  no operation moved by 1% of the time
where the time goes in v5:
time: 41.5 us; the launch traced here: 41.4 us
  Pallas kernels  40.8 us (98%)
  local copies, waits for them, and re-layouts  0.62 us (1%)
    pallas_call x1, Pallas kernels, local(): pl.pallas_call(kernel, out_shape=jax.ShapeDtypeStruct((4, FEAT), jnp.floa...  40.8 us

profile of v5, /device:TPU:1, one launch (start us, length us, event | category | flops | bytes accessed | tf_op | source)
XLA Modules:
  0.0 41.4 jit_solution(6879155848941653496)
XLA Ops:
  0.0 40.8 %shard_map.28 = f32[4,2048]{1,0:T(4,128)S(1)} custom-call(bf16[1024,2048]{1,0:T(8,128)(2,1)} %inputs.1, bf16[128,2048]{1,0:T(8,128)(2,1)} %inducing.1), custom_call_target="tpu_custom_call" | custom-call | tf_op jit(solution)/shard_map/pallas_call | solution.py:318
  40.8 0.6 %copy.4 = f32[4,2048]{1,0:T(4,128)} copy(f32[4,2048]{1,0:T(4,128)S(1)} %shard_map.28) | data formatting | bytes 65536

commit v6 on v4

--- a/solution.py
+++ b/solution.py
@@ -42,15 +42,6 @@
 
     def wait_bytes(ref, sem):
         pltpu.make_async_copy(ref, ref, sem).wait()
-
-    load_i = pltpu.make_async_copy(inducing, i_buf, in_sem.at[CHUNKS])
-    load_i.start()
-    loads = []
-    for n in range(CHUNKS):
-        rows = pl.ds(CUTS[n], CUTS[n + 1] - CUTS[n])
-        load = pltpu.make_async_copy(inputs.at[rows], x_buf.at[rows], in_sem.at[n])
-        load.start()
-        loads.append(load)
 
     partner = (block_of(x, yh, 1 - c), dp)
     edge = (block_of(x, 1 - yh, c), dp)
@@ -63,6 +54,15 @@
     barrier = pltpu.get_barrier_semaphore()
     for device in near:
         signal(barrier, device)
+
+    load_i = pltpu.make_async_copy(inducing, i_buf, in_sem.at[CHUNKS])
+    load_i.start()
+    loads = []
+    for n in range(CHUNKS):
+        rows = pl.ds(CUTS[n], CUTS[n + 1] - CUTS[n])
+        load = pltpu.make_async_copy(inputs.at[rows], x_buf.at[rows], in_sem.at[n])
+        load.start()
+        loads.append(load)
 
     def make_chunk(n):
         rows = pl.ds(CUTS[n], CUTS[n + 1] - CUTS[n])

time: 41.6 us -> 41.5 us (level)
  no operation moved by 1% of the time
where the time goes in v6:
time: 41.5 us; the launch traced here: 41.4 us
  Pallas kernels  40.8 us (98%)
  local copies, waits for them, and re-layouts  0.62 us (1%)
    pallas_call x1, Pallas kernels, local(): pl.pallas_call(kernel, out_shape=jax.ShapeDtypeStruct((4, FEAT), jnp.floa...  40.8 us

profile of v6, /device:TPU:1, one launch (start us, length us, event | category | flops | bytes accessed | tf_op | source)
XLA Modules:
  0.0 41.4 jit_solution(13700062084475334236)
XLA Ops:
  0.0 40.8 %shard_map.28 = f32[4,2048]{1,0:T(4,128)S(1)} custom-call(bf16[1024,2048]{1,0:T(8,128)(2,1)} %inputs.1, bf16[128,2048]{1,0:T(8,128)(2,1)} %inducing.1), custom_call_target="tpu_custom_call" | custom-call | tf_op jit(solution)/shard_map/pallas_call | solution.py:317
  40.8 0.6 %copy.4 = f32[4,2048]{1,0:T(4,128)} copy(f32[4,2048]{1,0:T(4,128)S(1)} %shard_map.28) | data formatting | bytes 65536
